TPU v7x, 32 devices: a whole 2x2x4 slice. The times are simulated.
32 devices in a mesh: dp: 4 (over z), ctx: 4 (over x, core), fsdp: 2 (over y).
Axes of the slice: x: 2, y: 2, z: 4, core: 2. Of those that a mesh axis runs over, the one named last changes fastest.
Arguments:
- hidden: bfloat16 [8, 1024, 2048], P(('dp', 'fsdp'), 'ctx'), may hold values from -6 to 6
- segment_ids: int32 [8, 1024], P(('dp', 'fsdp')), may hold values from 0 to 4, as said below
- positions: int32 [8, 1024], P(('dp', 'fsdp')), may hold values from 0 to 799, as said below
- attn_gain: bfloat16 [2048], P(('dp', 'ctx', 'fsdp')), may hold values from 0.099609375 to 1.8984375
- w_query: bfloat16 [2048, 2048], P(('dp', 'fsdp'), 'ctx'), may hold values from -0.015625 to 0.015625
- w_key: bfloat16 [2048, 2048], P(('dp', 'fsdp'), 'ctx'), may hold values from -0.125 to 0.125
- w_value: bfloat16 [2048, 2048], P(('dp', 'fsdp'), 'ctx'), may hold values from -0.125 to 0.125
- w_attn_out: bfloat16 [2048, 2048], P('ctx', ('dp', 'fsdp')), may hold values from -1.5 to 1.5
- rel_table: bfloat16 [1024], P(('dp', 'ctx', 'fsdp')), may hold values from -4 to 4
- ffn_gain: bfloat16 [2048], P(('dp', 'ctx', 'fsdp')), may hold values from 0.099609375 to 1.8984375
- w_gate: bfloat16 [2048, 5120], P(('dp', 'fsdp'), 'ctx'), may hold values from -0.125 to 0.125
- w_up: bfloat16 [2048, 5120], P(('dp', 'fsdp'), 'ctx'), may hold values from -0.125 to 0.125
- w_down: bfloat16 [5120, 2048], P('ctx', ('dp', 'fsdp')), may hold values from -0.078125 to 0.078125
- cotangent: bfloat16 [8, 1024, 2048], P(('dp', 'fsdp'), 'ctx'), may hold values from -6 to 6
Outputs:
- output: bfloat16 [8, 1024, 2048], P(('dp', 'fsdp'), 'ctx')
- grad_hidden: float32 [8, 1024, 2048], P(('dp', 'fsdp'), 'ctx')
- grad_attn_gain: float32 [2048], P(('dp', 'ctx', 'fsdp'))
- grad_query: float32 [2048, 2048], P(('dp', 'fsdp'), 'ctx')
- grad_key: float32 [2048, 2048], P(('dp', 'fsdp'), 'ctx')
- grad_value: float32 [2048, 2048], P(('dp', 'fsdp'), 'ctx')
- grad_attn_out: float32 [2048, 2048], P('ctx', ('dp', 'fsdp'))
- bias_table_gradient: float32 [1024], P(('dp', 'ctx', 'fsdp'))
- grad_ffn_gain: float32 [2048], P(('dp', 'ctx', 'fsdp'))
- grad_gate: float32 [2048, 5120], P(('dp', 'fsdp'), 'ctx')
- grad_up: float32 [2048, 5120], P(('dp', 'fsdp'), 'ctx')
- grad_down: float32 [5120, 2048], P('ctx', ('dp', 'fsdp'))
Inputs may be any that keep to these rules, and one draw needn't show every extreme that they name: `segment_ids`: within each sequence the ids number its documents from 0 and never fall. One document of each sequence, its first or its second, holds exactly 800 tokens; every other document holds 60 to 800 tokens, except the last one, which the end of the sequence may cut short. `positions`: 0 at a document's first token and rising by one along it, consistent with segment_ids.
All inputs are finite; a program needn't handle non-finite values.
Results may differ from a plain program's by a relative error of at most 0.018.
Values may be sent and summed in bfloat16 or wider, within the bound.
A program may use at most 256 MiB of HBM per device.

v0:
```python
import jax
import jax.numpy as jnp
from jax import lax
from jax.sharding import PartitionSpec as P

H = 32
DH = 64
NB = 32
QB = 512
EPSILON = 1e-06
THRESHOLDS = (12, 16, 23, 32, 46, 64, 91)
MASKED = -1e30


def rms_norm(values, gain):
    return values * lax.rsqrt(jnp.mean(values * values, axis=-1, keepdims=True) + EPSILON) * gain


def gelu_tanh(values):
    return (
        0.5
        * values
        * (1.0 + jnp.tanh(0.7978845608028654 * (values + 0.044715 * values * values * values)))
    )


def bucket_table(query_pos, key_pos):
    relative = key_pos[None, :] - query_pos[:, None]
    distance = jnp.abs(relative)
    log_bucket = 8 + sum(((distance >= threshold).astype(jnp.int32) for threshold in THRESHOLDS))
    bucket = jnp.where(distance < 8, distance, log_bucket)
    return bucket + 16 * (relative > 0).astype(jnp.int32)


def gather_attention(w_query, w_key, w_value, w_attn_out):
    return (
        lax.all_gather(w_query, ("dp", "fsdp"), axis=0, tiled=True),
        lax.all_gather(w_key, ("dp", "fsdp"), axis=0, tiled=True),
        lax.all_gather(w_value, ("dp", "fsdp"), axis=0, tiled=True),
        lax.all_gather(w_attn_out, ("dp", "fsdp"), axis=1, tiled=True),
    )


def gather_feedforward(w_gate, w_up, w_down):
    return (
        lax.all_gather(w_gate, ("dp", "fsdp"), axis=0, tiled=True),
        lax.all_gather(w_up, ("dp", "fsdp"), axis=0, tiled=True),
        lax.all_gather(w_down, ("dp", "fsdp"), axis=1, tiled=True),
    )


def block_masks(segment_row, position_row, start):
    query_pos = lax.dynamic_slice_in_dim(position_row, start, QB)
    query_seg = lax.dynamic_slice_in_dim(segment_row, start, QB)
    buckets = bucket_table(query_pos, position_row)
    one_hot = (buckets[None] == jnp.arange(NB, dtype=jnp.int32)[:, None, None]).astype(jnp.bfloat16)
    same_doc = query_seg[:, None] == segment_row[None, :]
    return (one_hot, same_doc)


def block_scores(query_block, key_rows, table_local, one_hot, same_doc):
    attention_scores = jnp.einsum(
        "ihd,jhd->hij", query_block, key_rows, preferred_element_type=jnp.float32
    )
    attention_scores = attention_scores + jnp.einsum(
        "bij,bh->hij", one_hot, table_local, preferred_element_type=jnp.float32
    )
    return jnp.where(same_doc[None], attention_scores, MASKED)


def layer_forward(tokens, small_set, attn_set, ffn_set, segment_row, position_row):
    attn_gain, ffn_gain, table_flat = small_set
    w_query, w_key, w_value, w_attn_out = attn_set
    w_gate, w_up, w_down = ffn_set
    heads_here = w_query.shape[1] // DH
    head_start = lax.axis_index("ctx") * heads_here
    table_local = lax.dynamic_slice_in_dim(table_flat.reshape(NB, H), head_start, heads_here, 1)
    normalized_rows, attn_back = jax.vjp(rms_norm, tokens, attn_gain.astype(jnp.float32))
    normed_rows = lax.all_gather(normalized_rows.astype(jnp.bfloat16), "ctx", axis=0, tiled=True)
    seq_len = normed_rows.shape[0]
    queries = (
        jnp.dot(normed_rows, w_query, preferred_element_type=jnp.float32)
        .astype(jnp.bfloat16)
        .reshape(seq_len, heads_here, DH)
    )
    key_rows = (
        jnp.dot(normed_rows, w_key, preferred_element_type=jnp.float32)
        .astype(jnp.bfloat16)
        .reshape(seq_len, heads_here, DH)
    )
    value_rows = (
        jnp.dot(normed_rows, w_value, preferred_element_type=jnp.float32)
        .astype(jnp.bfloat16)
        .reshape(seq_len, heads_here, DH)
    )
    starts = jnp.arange(seq_len // QB, dtype=jnp.int32) * QB

    def forward_block(start):
        one_hot, same_doc = block_masks(segment_row, position_row, start)
        query_block = lax.dynamic_slice_in_dim(queries, start, QB, 0)
        attention_scores = block_scores(query_block, key_rows, table_local, one_hot, same_doc)
        row_peak = jnp.max(attention_scores, axis=-1, keepdims=True)
        lifted = jnp.exp(attention_scores - row_peak)
        row_total = jnp.sum(lifted, axis=-1, keepdims=True)
        prob_low = (lifted / row_total).astype(jnp.bfloat16)
        attended_part = jnp.einsum(
            "hij,jhd->ihd", prob_low, value_rows, preferred_element_type=jnp.float32
        )
        return (attended_part, row_peak + jnp.log(row_total))

    attended, log_total = lax.map(forward_block, starts)
    attended_low = attended.reshape(seq_len, heads_here * DH).astype(jnp.bfloat16)
    attn_term = jnp.dot(attended_low, w_attn_out, preferred_element_type=jnp.float32)
    residual = tokens + lax.psum_scatter(attn_term, "ctx", scatter_dimension=0, tiled=True)
    normed_ffn, ffn_back = jax.vjp(rms_norm, residual, ffn_gain.astype(jnp.float32))
    ffn_rows = lax.all_gather(normed_ffn.astype(jnp.bfloat16), "ctx", axis=0, tiled=True)
    gate_value = jnp.dot(ffn_rows, w_gate, preferred_element_type=jnp.float32)
    up_value = jnp.dot(ffn_rows, w_up, preferred_element_type=jnp.float32)
    gelu_gate, gelu_back = jax.vjp(gelu_tanh, gate_value)
    ffn_hidden = (gelu_gate * up_value).astype(jnp.bfloat16)
    down_term = jnp.dot(ffn_hidden, w_down, preferred_element_type=jnp.float32)
    result = residual + lax.psum_scatter(
        down_term.astype(jnp.bfloat16), "ctx", scatter_dimension=0, tiled=True
    ).astype(jnp.float32)
    stored = (
        attn_back,
        normed_rows,
        queries,
        key_rows,
        value_rows,
        table_local,
        head_start,
        starts,
        log_total,
        attended_low,
        ffn_back,
        ffn_rows,
        up_value,
        gelu_gate,
        gelu_back,
        ffn_hidden,
    )
    return (result, stored)


def on_device(
    hidden,
    segment_ids,
    positions,
    attn_gain,
    w_query,
    w_key,
    w_value,
    w_attn_out,
    rel_table,
    ffn_gain,
    w_gate,
    w_up,
    w_down,
    cotangent,
):
    tokens = hidden[0].astype(jnp.float32)
    segment_row = segment_ids[0]
    position_row = positions[0]
    small_set = (
        lax.all_gather(attn_gain, ("dp", "ctx", "fsdp"), axis=0, tiled=True),
        lax.all_gather(ffn_gain, ("dp", "ctx", "fsdp"), axis=0, tiled=True),
        lax.all_gather(rel_table, ("dp", "ctx", "fsdp"), axis=0, tiled=True),
    )
    attn_set = gather_attention(w_query, w_key, w_value, w_attn_out)
    ffn_set = gather_feedforward(w_gate, w_up, w_down)
    result, unused_stored = layer_forward(
        tokens, small_set, attn_set, ffn_set, segment_row, position_row
    )
    back_attn = gather_attention(w_query, w_key, w_value, w_attn_out)
    back_ffn = gather_feedforward(w_gate, w_up, w_down)
    recomputed, stored = layer_forward(
        tokens, small_set, back_attn, back_ffn, segment_row, position_row
    )
    (
        attn_back,
        normed_rows,
        queries,
        key_rows,
        value_rows,
        table_local,
        head_start,
        starts,
        log_total,
        attended_low,
        ffn_back,
        ffn_rows,
        up_value,
        gelu_gate,
        gelu_back,
        ffn_hidden,
    ) = stored
    full_query, full_key, full_value, full_attn_out = back_attn
    full_gate, full_up, full_down = back_ffn
    seq_len = normed_rows.shape[0]
    heads_here = queries.shape[1]
    grad_rows = lax.all_gather(cotangent[0], "ctx", axis=0, tiled=True)
    grad_w_down = jnp.einsum("tf,td->fd", ffn_hidden, grad_rows, preferred_element_type=jnp.float32)
    grad_hidden_ffn = jnp.einsum(
        "td,fd->tf", grad_rows, full_down, preferred_element_type=jnp.float32
    )
    up_value_gradient = (grad_hidden_ffn * gelu_gate).astype(jnp.bfloat16)
    grad_gate_value = gelu_back(grad_hidden_ffn * up_value)[0].astype(jnp.bfloat16)
    grad_w_gate = jnp.einsum(
        "td,tf->df", ffn_rows, grad_gate_value, preferred_element_type=jnp.float32
    )
    grad_w_up = jnp.einsum(
        "td,tf->df", ffn_rows, up_value_gradient, preferred_element_type=jnp.float32
    )
    ffn_normed_term = jnp.einsum(
        "tf,df->td", grad_gate_value, full_gate, preferred_element_type=jnp.float32
    )
    ffn_normed_term = ffn_normed_term + jnp.einsum(
        "tf,df->td", up_value_gradient, full_up, preferred_element_type=jnp.float32
    )
    grad_normed_ffn = lax.psum_scatter(ffn_normed_term, "ctx", scatter_dimension=0, tiled=True)
    grad_residual_norm, grad_ffn_gain = ffn_back(grad_normed_ffn)
    grad_residual = cotangent[0].astype(jnp.float32) + grad_residual_norm
    ffn_sums = (
        lax.psum_scatter(
            grad_w_gate.astype(jnp.bfloat16), ("dp", "fsdp"), scatter_dimension=0, tiled=True
        ).astype(jnp.float32),
        lax.psum_scatter(
            grad_w_up.astype(jnp.bfloat16), ("dp", "fsdp"), scatter_dimension=0, tiled=True
        ).astype(jnp.float32),
        lax.psum_scatter(
            grad_w_down.astype(jnp.bfloat16), ("dp", "fsdp"), scatter_dimension=1, tiled=True
        ).astype(jnp.float32),
    )
    branch_rows = lax.all_gather(grad_residual.astype(jnp.bfloat16), "ctx", axis=0, tiled=True)
    grad_w_attn_out = jnp.einsum(
        "ti,td->id", attended_low, branch_rows, preferred_element_type=jnp.float32
    )
    grad_attended = jnp.einsum(
        "td,id->ti", branch_rows, full_attn_out, preferred_element_type=jnp.float32
    )
    grad_attended = grad_attended.astype(jnp.bfloat16).reshape(seq_len, heads_here, DH)

    def backward_block(operands):
        start, block_total = operands
        one_hot, same_doc = block_masks(segment_row, position_row, start)
        query_block = lax.dynamic_slice_in_dim(queries, start, QB, 0)
        grad_part = lax.dynamic_slice_in_dim(grad_attended, start, QB, 0)
        attention_scores = block_scores(query_block, key_rows, table_local, one_hot, same_doc)
        weights = jnp.exp(attention_scores - block_total)
        prob_low = weights.astype(jnp.bfloat16)
        grad_probs = jnp.einsum(
            "ihd,jhd->hij", grad_part, value_rows, preferred_element_type=jnp.float32
        )
        centred = grad_probs - jnp.sum(weights * grad_probs, axis=-1, keepdims=True)
        grad_scores = (weights * centred).astype(jnp.bfloat16)
        grad_query_part = jnp.einsum(
            "hij,jhd->ihd", grad_scores, key_rows, preferred_element_type=jnp.float32
        )
        grad_key_part = jnp.einsum(
            "hij,ihd->jhd", grad_scores, query_block, preferred_element_type=jnp.float32
        )
        grad_value_part = jnp.einsum(
            "hij,ihd->jhd", prob_low, grad_part, preferred_element_type=jnp.float32
        )
        grad_bias_part = jnp.einsum(
            "hij,bij->bh", grad_scores, one_hot, preferred_element_type=jnp.float32
        )
        return (grad_query_part, grad_key_part, grad_value_part, grad_bias_part)

    query_blocks, key_blocks, value_blocks, bias_blocks = lax.map(
        backward_block, (starts, log_total)
    )
    grad_queries_low = query_blocks.reshape(seq_len, heads_here * DH).astype(jnp.bfloat16)
    grad_keys_low = (
        jnp.sum(key_blocks, axis=0).reshape(seq_len, heads_here * DH).astype(jnp.bfloat16)
    )
    grad_values_low = (
        jnp.sum(value_blocks, axis=0).reshape(seq_len, heads_here * DH).astype(jnp.bfloat16)
    )
    grad_w_query = jnp.einsum(
        "td,te->de", normed_rows, grad_queries_low, preferred_element_type=jnp.float32
    )
    grad_w_key = jnp.einsum(
        "td,te->de", normed_rows, grad_keys_low, preferred_element_type=jnp.float32
    )
    grad_w_value = jnp.einsum(
        "td,te->de", normed_rows, grad_values_low, preferred_element_type=jnp.float32
    )
    normed_term = jnp.einsum(
        "te,de->td", grad_queries_low, full_query, preferred_element_type=jnp.float32
    )
    normed_term = normed_term + jnp.einsum(
        "te,de->td", grad_keys_low, full_key, preferred_element_type=jnp.float32
    )
    normed_term = normed_term + jnp.einsum(
        "te,de->td", grad_values_low, full_value, preferred_element_type=jnp.float32
    )
    grad_normed = lax.psum_scatter(
        normed_term.astype(jnp.bfloat16), "ctx", scatter_dimension=0, tiled=True
    ).astype(jnp.float32)
    token_norm_gradient, grad_attn_gain = attn_back(grad_normed)
    grad_tokens = grad_residual + token_norm_gradient
    attn_sums = (
        lax.psum_scatter(
            grad_w_query.astype(jnp.bfloat16), ("dp", "fsdp"), scatter_dimension=0, tiled=True
        ).astype(jnp.float32),
        lax.psum_scatter(
            grad_w_key.astype(jnp.bfloat16), ("dp", "fsdp"), scatter_dimension=0, tiled=True
        ).astype(jnp.float32),
        lax.psum_scatter(
            grad_w_value.astype(jnp.bfloat16), ("dp", "fsdp"), scatter_dimension=0, tiled=True
        ).astype(jnp.float32),
        lax.psum_scatter(
            grad_w_attn_out.astype(jnp.bfloat16), ("dp", "fsdp"), scatter_dimension=1, tiled=True
        ).astype(jnp.float32),
    )
    bias_sum = jnp.sum(bias_blocks, axis=0)
    table_term = lax.dynamic_update_slice(
        jnp.zeros((NB, H), jnp.float32), bias_sum, (jnp.int32(0), head_start)
    )
    small_sums = (
        lax.psum_scatter(grad_attn_gain, ("dp", "ctx", "fsdp"), scatter_dimension=0, tiled=True),
        lax.psum_scatter(grad_ffn_gain, ("dp", "ctx", "fsdp"), scatter_dimension=0, tiled=True),
        lax.psum_scatter(
            table_term.reshape(NB * H), ("dp", "ctx", "fsdp"), scatter_dimension=0, tiled=True
        ),
    )
    return (
        result[None].astype(jnp.bfloat16),
        grad_tokens[None],
        small_sums[0],
        attn_sums[0],
        attn_sums[1],
        attn_sums[2],
        attn_sums[3],
        small_sums[2],
        small_sums[1],
        ffn_sums[0],
        ffn_sums[1],
        ffn_sums[2],
    )


def solution(mesh):
    in_specs = (
        P(("dp", "fsdp"), "ctx", None),
        P(("dp", "fsdp"), None),
        P(("dp", "fsdp"), None),
        P(("dp", "ctx", "fsdp")),
        P(("dp", "fsdp"), "ctx"),
        P(("dp", "fsdp"), "ctx"),
        P(("dp", "fsdp"), "ctx"),
        P("ctx", ("dp", "fsdp")),
        P(("dp", "ctx", "fsdp")),
        P(("dp", "ctx", "fsdp")),
        P(("dp", "fsdp"), "ctx"),
        P(("dp", "fsdp"), "ctx"),
        P("ctx", ("dp", "fsdp")),
        P(("dp", "fsdp"), "ctx", None),
    )
    out_specs = (
        P(("dp", "fsdp"), "ctx", None),
        P(("dp", "fsdp"), "ctx", None),
        P(("dp", "ctx", "fsdp")),
        P(("dp", "fsdp"), "ctx"),
        P(("dp", "fsdp"), "ctx"),
        P(("dp", "fsdp"), "ctx"),
        P("ctx", ("dp", "fsdp")),
        P(("dp", "ctx", "fsdp")),
        P(("dp", "ctx", "fsdp")),
        P(("dp", "fsdp"), "ctx"),
        P(("dp", "fsdp"), "ctx"),
        P("ctx", ("dp", "fsdp")),
    )
    return jax.shard_map(
        on_device, mesh=mesh, in_specs=in_specs, out_specs=out_specs, check_vma=False
    )
```

profile of v0, /device:TPU:0, one launch (start us, length us, event | category | flops | bytes accessed | tf_op | source)
XLA Modules:
  0.0 1926.7 jit_solution(9889861834597921747)
XLA Ops:
  10.6 43.6 %all-reduce.8 = (bf16[2048]{0:T(1024)(128)(2,1)}, bf16[2048]{0:T(1024)(128)(2,1)S(1)}, bf16[32,32]{1,0:T(8,128)(2,1)S(1)}) all-reduce(bf16[2048]{0:T(1024)(128)(2,1)S(1)} %dynamic-update-slice.2, bf16[2048]{0:T(1024)(128)(2,1)S(1)} %dynamic-update-slice, ...), channel_id=1, replica_groups=mesh['dp'=4,'ctx'=4,'fsdp'=2] {'dp','ctx','fsdp'}, use_global_device_ids=true, to_apply=%add.2 | all-reduce | flops 5120 | bytes 20480
  63.3 35.1 %all-gather.14.cloned.1.call-done = bf16[1024,2048]{1,0:T(8,128)(2,1)} async-done(((bf16[256,2048]{1,0:T(8,128)(2,1)}), bf16[1024,2048]{1,0:T(8,128)(2,1)}) %all-gather.14.cloned.1.call-update) | async-done | bytes 4194320 | tf_op jit(solution)/shard_map/all_gather | solution.py:79
  104.7 45.3 %all-gather.18.cloned.1.call-done = bf16[2048,512]{1,0:T(8,128)(2,1)} async-done(((bf16[256,512]{1,0:T(8,128)(2,1)}), bf16[2048,512]{1,0:T(8,128)(2,1)}) %all-gather.18.cloned.1.call-update) | async-done | bytes 2097168 | tf_op jit(solution)/shard_map/all_gather | solution.py:38
  156.1 43.6 %all-gather.16.cloned.1.call-done = bf16[2048,512]{1,0:T(8,128)(2,1)} async-done(((bf16[256,512]{1,0:T(8,128)(2,1)}), bf16[2048,512]{1,0:T(8,128)(2,1)}) %all-gather.16.cloned.1.call-update) | async-done | bytes 2097168 | tf_op jit(solution)/shard_map/all_gather | solution.py:37
  206.1 128.6 %while.39 = (s32[]{:T(128)}, bf16[2,512,8,64]{1,3,2,0:T(8,128)(2,1)S(1)}, f32[2,8,512,1]{2,1,3,0:T(8,128)S(1)}, s32[2]{0:T(128)S(1)}, s32[1024]{0:T(1024)S(1)}, ...) while((s32[]{:T(128)}, ...), condition=%wide.region_11.12_spmd, body=%wide.region_8.11_spmd.sunk | while | flops 1407709184 | bytes 160060144 | solution.py:111
  238.1 24.2 %fusion.226 = (f32[8,512]{1,0:T(8,128)S(1)}, f32[8,512,1024]{2,1,0:T(8,128)}) fusion(f32[512,1024,8]{1,2,0:T(8,128)} %fusion.225, bf16[1024,8,64]{0,2,1:T(8,128)(2,1)} %get-tuple-element.720, bf16[1024,8,64]{0,2,1:T(8,128)(2,1)} %get-tuple-element.719, s32[]{:T(128)S(6)} %select_n.81, pred[512,1024]{1,0:T(8,128)(4,1)S(1)} %broadcast_compare_fusion.7), kind=kOutput, calls=%fused_computation.180.clone.1 | convolution fusion | flops 549449728 | bytes 35667972 | tf_op jit(solution)/shard_map/while/body/eval_jaxpr/ihd,jhd->hij/dot_general | solution.py:62
  295.1 24.1 %fusion.226 = (f32[8,512]{1,0:T(8,128)S(1)}, f32[8,512,1024]{2,1,0:T(8,128)}) fusion(f32[512,1024,8]{1,2,0:T(8,128)} %fusion.225, bf16[1024,8,64]{0,2,1:T(8,128)(2,1)} %get-tuple-element.720, bf16[1024,8,64]{0,2,1:T(8,128)(2,1)} %get-tuple-element.719, s32[]{:T(128)S(6)} %select_n.81, pred[512,1024]{1,0:T(8,128)(4,1)S(1)} %broadcast_compare_fusion.7), kind=kOutput, calls=%fused_computation.180.clone.1 | convolution fusion | flops 549449728 | bytes 35667972 | tf_op jit(solution)/shard_map/while/body/eval_jaxpr/ihd,jhd->hij/dot_general | solution.py:62
  344.5 69.5 %reduce-scatter.17.cloned.1.call-done = f32[256,2048]{1,0:T(8,128)} async-done(((f32[1024,2048]{1,0:T(8,128)}), f32[256,2048]{1,0:T(8,128)}) %reduce-scatter.17.cloned.1.call-update) | async-done | bytes 2097168 | tf_op jit(solution)/shard_map/reduce_scatter | solution.py:114
  419.9 142.7 %while.38 = (s32[]{:T(128)}, bf16[2,512,8,64]{1,3,2,0:T(8,128)(2,1)S(1)}, s32[2]{0:T(128)S(1)}, s32[1024]{0:T(1024)S(1)}, s32[1,1024]{1,0:T(1,128)S(1)}, /*index...) while((s32[]{:T(128)}, ...), condition=%wide.region_4.5_spmd, body=%wide.region_1.4_spmd.sunk | while | flops 1403525120 | bytes 109630152 | solution.py:111
  437.8 23.7 %fusion.218 = f32[8,512,1024]{2,1,0:T(8,128)} fusion(f32[512,1024,8]{1,2,0:T(8,128)} %fusion.217, bf16[1024,8,64]{0,2,1:T(8,128)(2,1)} %get-tuple-element.762, pred[512,1024]{1,0:T(8,128)(4,1)S(1)} %broadcast_compare_fusion.6, bf16[1024,8,64]{0,2,1:T(8,128)(2,1)} %get-tuple-element.761, s32[]{:T(128)S(6)} %select_n.79), kind=kOutput, calls=%fused_computation.5.clone.1 | convolution fusion | flops 545259520 | bytes 35651588 | tf_op jit(solution)/shard_map/while/body/eval_jaxpr/ihd,jhd->hij/dot_general | solution.py:62
  507.9 25.0 %fusion.218 = f32[8,512,1024]{2,1,0:T(8,128)} fusion(f32[512,1024,8]{1,2,0:T(8,128)} %fusion.217, bf16[1024,8,64]{0,2,1:T(8,128)(2,1)} %get-tuple-element.762, pred[512,1024]{1,0:T(8,128)(4,1)S(1)} %broadcast_compare_fusion.6, bf16[1024,8,64]{0,2,1:T(8,128)(2,1)} %get-tuple-element.761, s32[]{:T(128)S(6)} %select_n.79), kind=kOutput, calls=%fused_computation.5.clone.1 | convolution fusion | flops 545259520 | bytes 35651588 | tf_op jit(solution)/shard_map/while/body/eval_jaxpr/ihd,jhd->hij/dot_general | solution.py:62
  546.8 15.3 fusion.220
  580.3 46.1 %all-gather.26.cloned.1.call-done = bf16[2048,1280]{1,0:T(8,128)(2,1)} async-done(((bf16[256,1280]{1,0:T(8,128)(2,1)}), bf16[2048,1280]{1,0:T(8,128)(2,1)}) %all-gather.26.cloned.1.call-update) | async-done | bytes 5242896 | tf_op jit(solution)/shard_map/all_gather | solution.py:46
  636.8 23.8 %all-gather.36.cloned.1.call-done = bf16[1,1024,2048]{2,1,0:T(8,128)(2,1)} async-done(((bf16[1,256,2048]{2,1,0:T(8,128)(2,1)}), bf16[1,1024,2048]{2,1,0:T(8,128)(2,1)}) %all-gather.36.cloned.1.call-update) | async-done | bytes 4194320 | tf_op jit(solution)/shard_map/all_gather | solution.py:202
  660.6 89.5 %all-gather.30.cloned.1.call-done = bf16[1280,2048]{1,0:T(8,128)(2,1)} async-done(((bf16[1280,256]{1,0:T(8,128)(2,1)}), bf16[1280,2048]{1,0:T(8,128)(2,1)}) %all-gather.30.cloned.1.call-update) | async-done | bytes 5242896 | tf_op jit(solution)/shard_map/all_gather | solution.py:48
  750.1 16.3 multiply_convert_fusion.2
  782.9 39.8 %reduce-scatter.13.cloned.1.call-done = f32[256,2048]{1,0:T(8,128)} async-done(((f32[1024,2048]{1,0:T(8,128)}), f32[256,2048]{1,0:T(8,128)}) %reduce-scatter.13.cloned.1.call-update) | async-done | bytes 2097168 | tf_op jit(solution)/shard_map/reduce_scatter | solution.py:114
  822.7 74.3 %reduce-scatter.19.cloned.1.call-done = f32[256,2048]{1,0:T(8,128)} async-done(((f32[1024,2048]{1,0:T(8,128)}), f32[256,2048]{1,0:T(8,128)}) %reduce-scatter.19.cloned.1.call-update) | async-done | bytes 2097168 | tf_op jit(solution)/shard_map/reduce_scatter | solution.py:221
  902.9 34.5 %all-gather.34.cloned.1.call-done = bf16[1024,2048]{1,0:T(8,128)(2,1)} async-done(((bf16[256,2048]{1,0:T(8,128)(2,1)}), bf16[1024,2048]{1,0:T(8,128)(2,1)}) %all-gather.34.cloned.1.call-update) | async-done | bytes 4194320 | tf_op jit(solution)/shard_map/all_gather | solution.py:235
  944.8 214.2 %while.40 = (s32[]{:T(128)}, bf16[2,512,8,64]{1,3,2,0:T(8,128)(2,1)}, f32[2,1024,8,64]{1,3,2,0:T(8,128)}, f32[2,1024,8,64]{1,3,2,0:T(8,128)}, f32[2,32,8]{1,2,0:...) while((s32[]{:T(128)}, ...), condition=%wide.region_18.19_spmd, body=%wide.region_16.18_spmd.sunk | while | flops 3307728896 | bytes 294757248 | solution.py:271
  990.7 25.9 %multiply_reduce_fusion.6 = (f32[8,512]{1,0:T(8,128)S(1)}, f32[8,512,1024]{2,1,0:T(8,128)}) fusion(f32[8,512,1024]{2,1,0:T(8,128)} %fusion.240, f32[8,512]{1,0:T(8,128)S(1)} %dynamic-slice_bitcast_fusion.2, f32[512,1024,8]{1,2,0:T(8,128)} %fusion.242, bf16[1024,8,64]{0,2,1:T(8,128)(2,1)} %get-tuple-element.817, ...), kind=kOutput, calls=%fused_computation.64.clone.1 | convolution fusion | flops 557838336 | bytes 52461572 | tf_op jit(solution)/shard_map/while/body/eval_jaxpr/ihd,jhd->hij/dot_general | solution.py:62
  1085.0 25.9 %multiply_reduce_fusion.6 = (f32[8,512]{1,0:T(8,128)S(1)}, f32[8,512,1024]{2,1,0:T(8,128)}) fusion(f32[8,512,1024]{2,1,0:T(8,128)} %fusion.240, f32[8,512]{1,0:T(8,128)S(1)} %dynamic-slice_bitcast_fusion.2, f32[512,1024,8]{1,2,0:T(8,128)} %fusion.242, bf16[1024,8,64]{0,2,1:T(8,128)(2,1)} %get-tuple-element.817, ...), kind=kOutput, calls=%fused_computation.64.clone.1 | convolution fusion | flops 557838336 | bytes 52461572 | tf_op jit(solution)/shard_map/while/body/eval_jaxpr/ihd,jhd->hij/dot_general | solution.py:62
  1182.4 44.0 %reduce-scatter.21.cloned.1.call-done = bf16[256,2048]{1,0:T(8,128)(2,1)} async-done(((bf16[1024,2048]{1,0:T(8,128)(2,1)}), bf16[256,2048]{1,0:T(8,128)(2,1)}) %reduce-scatter.21.cloned.1.call-update) | async-done | bytes 1048592 | tf_op jit(solution)/shard_map/reduce_scatter | solution.py:299
  1302.5 19.9 %convolution_convert_fusion.3 = bf16[1024,2048]{1,0:T(8,128)(2,1)} fusion(bf16[1280,2048]{1,0:T(8,128)(2,1)} %all-gather.30.cloned.1.call-done, f32[1024,1280]{1,0:T(8,128)} %fusion.113, bf16[1024,2048]{1,0:T(8,128)(2,1)} %all-gather.24.cloned.1.call-done, bf16[2048,1280]{1,0:T(8,128)(2,1)} %all-gather.28.cloned.1.call-done), kind=kOutput, calls=%fused_computation.131 | convolution fusion | flops 10752622592 | bytes 24117248 | tf_op jit(solution)/shard_map/dot_general | solution.py:121
  1322.5 53.3 %reduce-scatter.35.cloned.1.call-done = bf16[1280,256]{1,0:T(8,128)(2,1)} async-done(((bf16[1280,2048]{1,0:T(8,128)(2,1)}), bf16[1280,256]{1,0:T(8,128)(2,1)}) %reduce-scatter.35.cloned.1.call-update) | async-done | bytes 655376 | tf_op jit(solution)/shard_map/reduce_scatter | solution.py:231
  1378.1 103.7 %reduce-scatter.33.cloned.1.call-done = bf16[256,1280]{1,0:T(8,128)(2,1)} async-done(((bf16[2048,1280]{1,0:T(8,128)(2,1)}), bf16[256,1280]{1,0:T(8,128)(2,1)}) %reduce-scatter.33.cloned.1.call-update) | async-done | bytes 655376 | tf_op jit(solution)/shard_map/reduce_scatter | solution.py:228
  1484.0 103.9 %reduce-scatter.31.cloned.1.call-done = bf16[256,1280]{1,0:T(8,128)(2,1)} async-done(((bf16[2048,1280]{1,0:T(8,128)(2,1)}), bf16[256,1280]{1,0:T(8,128)(2,1)}) %reduce-scatter.31.cloned.1.call-update) | async-done | bytes 655376 | tf_op jit(solution)/shard_map/reduce_scatter | solution.py:225
  1590.5 68.9 %reduce-scatter.29.cloned.1.call-done = bf16[512,256]{1,0:T(8,128)(2,1)} async-done(((bf16[512,2048]{1,0:T(8,128)(2,1)}), bf16[512,256]{1,0:T(8,128)(2,1)}) %reduce-scatter.29.cloned.1.call-update) | async-done | bytes 262160 | tf_op jit(solution)/shard_map/reduce_scatter | solution.py:314
  1661.2 68.5 %reduce-scatter.23.cloned.1.call-done = bf16[256,512]{1,0:T(8,128)(2,1)} async-done(((bf16[2048,512]{1,0:T(8,128)(2,1)}), bf16[256,512]{1,0:T(8,128)(2,1)}) %reduce-scatter.23.cloned.1.call-update) | async-done | bytes 262160 | tf_op jit(solution)/shard_map/reduce_scatter | solution.py:305
  1731.5 68.5 %reduce-scatter.27.cloned.1.call-done = bf16[256,512]{1,0:T(8,128)(2,1)} async-done(((bf16[2048,512]{1,0:T(8,128)(2,1)}), bf16[256,512]{1,0:T(8,128)(2,1)}) %reduce-scatter.27.cloned.1.call-update) | async-done | bytes 262160 | tf_op jit(solution)/shard_map/reduce_scatter | solution.py:311
  1801.8 68.6 %reduce-scatter.25.cloned.1.call-done = bf16[256,512]{1,0:T(8,128)(2,1)} async-done(((bf16[2048,512]{1,0:T(8,128)(2,1)}), bf16[256,512]{1,0:T(8,128)(2,1)}) %reduce-scatter.25.cloned.1.call-update) | async-done | bytes 262160 | tf_op jit(solution)/shard_map/reduce_scatter | solution.py:308
  1872.2 40.0 %all-reduce.7 = (f32[2048]{0:T(1024)S(1)}, f32[1024]{0:T(1024)S(1)}, f32[2048]{0:T(1024)S(1)}) all-reduce(f32[2048]{0:T(1024)S(1)} %get-tuple-element.343, f32[1024]{0:T(1024)S(1)} %reshape.387, f32[2048]{0:T(1024)S(1)} %copy-done.31), channel_id=8, replica_groups=mesh['dp'=4,'ctx'=4,'fsdp'=2] {'dp','ctx','fsdp'}, use_global_device_ids=true, to_apply=%region_24.25.clone | all-reduce | flops 5120 | bytes 40960
  (302 shorter events, 493.4 us)
Async XLA Ops:
  7.2 56.2 %all-gather.20.cloned.1.call-start = ((), (), s32[]{:S(2)}) async-start(), calls=%async_computation.15 | async-start | bytes 2359296 | tf_op jit(solution)/shard_map/all_gather | solution.py:39
  7.9 90.6 %all-gather.14.cloned.1.call-start = ((), (), s32[]{:S(2)}) async-start(), calls=%async_computation.12 | async-start | bytes 5242880 | tf_op jit(solution)/shard_map/all_gather | solution.py:79
  59.4 90.5 %all-gather.18.cloned.1.call-start = ((), (), s32[]{:S(2)}) async-start(), calls=%async_computation.14 | async-start | bytes 2359296 | tf_op jit(solution)/shard_map/all_gather | solution.py:38
  60.1 139.6 %all-gather.16.cloned.1.call-start = ((), (), s32[]{:S(2)}) async-start(), calls=%async_computation.13 | async-start | bytes 2359296 | tf_op jit(solution)/shard_map/all_gather | solution.py:37
  60.7 275.3 %all-gather.22.cloned.1.call-start = ((), (), s32[]{:S(2)}) async-start(), calls=%async_computation.16 | async-start | bytes 2359296 | tf_op jit(solution)/shard_map/all_gather | solution.py:40
  61.3 352.7 %reduce-scatter.17.cloned.1.call-start = ((), (), s32[]{:S(2)}) async-start(), calls=%async_computation.23 | async-start | bytes 10485760 | tf_op jit(solution)/shard_map/reduce_scatter | solution.py:114
  343.7 226.2 %all-gather.28.cloned.1.call-start = ((), (), s32[]{:S(2)}) async-start(), calls=%async_computation.20 | async-start | bytes 5898240 | tf_op jit(solution)/shard_map/all_gather | solution.py:47
  344.5 225.5 %all-gather.32.cloned.1.call-start = ((), (), s32[]{:S(2)}) async-start(), calls=%async_computation.24 | async-start | bytes 5242880 | tf_op jit(solution)/shard_map/all_gather | solution.py:116
  344.5 73.1 %copy-start.26 = (f32[2048]{0:T(1024)}, f32[2048]{0:T(1024)S(1)}, u32[]{:S(2)}) copy-start(f32[2048]{0:T(1024)S(1)} %convert_element_type.321) | copy-start | bytes 24580
  417.7 208.8 %all-gather.26.cloned.1.call-start = ((), (), s32[]{:S(2)}) async-start(), calls=%async_computation.19 | async-start | bytes 5898240 | tf_op jit(solution)/shard_map/all_gather | solution.py:46
  418.4 242.2 %all-gather.36.cloned.1.call-start = ((), (), s32[]{:S(2)}) async-start(), calls=%async_computation.35 | async-start | bytes 5242880 | tf_op jit(solution)/shard_map/all_gather | solution.py:202
  419.0 331.1 %all-gather.30.cloned.1.call-start = ((), (), s32[]{:S(2)}) async-start(), calls=%async_computation.21 | async-start | bytes 5898240 | tf_op jit(solution)/shard_map/all_gather | solution.py:48
  419.7 403.0 %reduce-scatter.13.cloned.1.call-start = ((), (), s32[]{:S(2)}) async-start(), calls=%async_computation.17 | async-start | bytes 10485760 | tf_op jit(solution)/shard_map/reduce_scatter | solution.py:114
  569.8 327.2 %reduce-scatter.19.cloned.1.call-start = ((), (), s32[]{:S(2)}) async-start(), calls=%async_computation.25 | async-start | bytes 10485760 | tf_op jit(solution)/shard_map/reduce_scatter | solution.py:221
  782.8 114.2 %copy-start.3 = (bf16[1,256,2048]{2,1,0:T(8,128)(2,1)S(1)}, bf16[1,256,2048]{2,1,0:T(8,128)(2,1)}, u32[]{:S(2)}) copy-start(bf16[1,256,2048]{2,1,0:T(8,128)(2,1)} %param.20) | copy-start | bytes 3145732
  782.8 114.2 %copy-start.6 = (f32[256,2048]{1,0:T(8,128)S(1)}, f32[256,2048]{1,0:T(8,128)}, u32[]{:S(2)}) copy-start(f32[256,2048]{1,0:T(8,128)} %reduce-scatter.17.cloned.1.call-done) | copy-start | bytes 6291460
  782.8 114.2 %copy-start.27 = (f32[2048]{0:T(1024)S(1)}, f32[2048]{0:T(1024)}, u32[]{:S(2)}) copy-start(f32[2048]{0:T(1024)} %copy-done.26) | copy-start | bytes 24580
  782.8 114.2 %copy-start.33 = (f32[256]{0:T(256)S(1)}, f32[256]{0:T(256)}, u32[]{:S(2)}) copy-start(f32[256]{0:T(256)} %copy-done.32) | copy-start | bytes 3076
  782.8 118.2 %copy-start.42 = (f32[256]{0:T(256)S(1)}, f32[256]{0:T(256)}, u32[]{:S(2)}) copy-start(f32[256]{0:T(256)} %copy-done.41) | copy-start | bytes 3076
  782.8 154.7 %all-gather.34.cloned.1.call-start = ((), (), s32[]{:S(2)}) async-start(), calls=%async_computation.26 | async-start | bytes 5242880 | tf_op jit(solution)/shard_map/all_gather | solution.py:235
  902.9 323.5 %reduce-scatter.21.cloned.1.call-start = ((), (), s32[]{:S(2)}) async-start(), calls=%async_computation.27 | async-start | bytes 5242880 | tf_op jit(solution)/shard_map/reduce_scatter | solution.py:299
  1181.8 110.3 %all-gather.24.cloned.1.call-start = ((), (), s32[]{:S(2)}) async-start(), calls=%async_computation.18 | async-start | bytes 5242880 | tf_op jit(solution)/shard_map/all_gather | solution.py:116
  1234.7 141.1 %reduce-scatter.35.cloned.1.call-start = ((), (), s32[]{:S(2)}) async-start(), calls=%async_computation.34 | async-start | bytes 5898240 | tf_op jit(solution)/shard_map/reduce_scatter | solution.py:231
  1246.5 235.3 %reduce-scatter.33.cloned.1.call-start = ((), (), s32[]{:S(2)}) async-start(), calls=%async_computation.33 | async-start | bytes 5898240 | tf_op jit(solution)/shard_map/reduce_scatter | solution.py:228
  1256.4 331.5 %reduce-scatter.31.cloned.1.call-start = ((), (), s32[]{:S(2)}) async-start(), calls=%async_computation.32 | async-start | bytes 5898240 | tf_op jit(solution)/shard_map/reduce_scatter | solution.py:225
  1266.3 393.1 %reduce-scatter.29.cloned.1.call-start = ((), (), s32[]{:S(2)}) async-start(), calls=%async_computation.31 | async-start | bytes 2359296 | tf_op jit(solution)/shard_map/reduce_scatter | solution.py:314
  1273.4 456.3 %reduce-scatter.23.cloned.1.call-start = ((), (), s32[]{:S(2)}) async-start(), calls=%async_computation.28 | async-start | bytes 2359296 | tf_op jit(solution)/shard_map/reduce_scatter | solution.py:305
  1279.5 520.4 %reduce-scatter.27.cloned.1.call-start = ((), (), s32[]{:S(2)}) async-start(), calls=%async_computation.30 | async-start | bytes 2359296 | tf_op jit(solution)/shard_map/reduce_scatter | solution.py:311
  1285.8 584.6 %reduce-scatter.25.cloned.1.call-start = ((), (), s32[]{:S(2)}) async-start(), calls=%async_computation.29 | async-start | bytes 2359296 | tf_op jit(solution)/shard_map/reduce_scatter | solution.py:308
  1291.8 625.1 %reduce-scatter.15.cloned.1.call-start = ((), (), s32[]{:S(2)}) async-start(), calls=%async_computation.22 | async-start | bytes 5242880 | tf_op jit(solution)/shard_map/reduce_scatter | solution.py:122
  1322.5 549.7 %copy-start.31 = (f32[2048]{0:T(1024)S(1)}, f32[2048]{0:T(1024)}, u32[]{:S(2)}) copy-start(f32[2048]{0:T(1024)} %get-tuple-element.341) | copy-start | bytes 24580
  1322.5 594.5 %copy-start.9 = (f32[256,2048]{1,0:T(8,128)S(1)}, f32[256,2048]{1,0:T(8,128)}, u32[]{:S(2)}) copy-start(f32[256,2048]{1,0:T(8,128)} %reduce-scatter.13.cloned.1.call-done) | copy-start | bytes 6291460
  (48 other events, 790.9 us)
Sparse Core Ops, SparseCore 0:
  10.1 53.1 all-gather.19
  65.5 32.9 all-gather.13
  100.6 49.2 all-gather.17
  151.9 47.7 all-gather.15
  201.6 49.5 all-gather.21
  343.8 70.1 reduce-scatter.16
  416.5 86.3 all-gather.27
  505.1 32.5 all-gather.31
  540.1 86.2 all-gather.25
  627.9 32.6 all-gather.35
  662.9 87.2 all-gather.29
  752.7 69.9 reduce-scatter.12
  825.3 71.7 reduce-scatter.18
  903.0 34.4 all-gather.33
  1181.9 44.4 reduce-scatter.20
  1234.9 34.4 all-gather.23
  1272.8 102.9 reduce-scatter.34
  1379.3 102.4 reduce-scatter.32
  1485.4 102.4 reduce-scatter.30
  1591.3 68.0 reduce-scatter.28
  1662.9 66.7 reduce-scatter.22
  1733.2 66.7 reduce-scatter.26
  1803.5 66.8 reduce-scatter.24
  1872.8 44.1 reduce-scatter.14
where the time goes:
time: 1930 us
  waiting for transfers between devices  1090 us (56%)
  matrix products  520 us (27%)
  other arithmetic  126 us (7%)
  blocking collectives  83.6 us (4%)
  loops' own time  53 us (3%)
  local copies, waits for them, and re-layouts  36.1 us (2%)
    dot_general x6, matrix products, block_scores(): jnp.einsum('ihd,jhd->hij', query_block, key_rows, preferred_element_type=...  149 us
    reduce_scatter x2, waiting for transfers between devices, layer_forward(): lax.psum_scatter(attn_term, 'ctx', scatter_dimension=0, tiled=True)  109 us
    reduce_scatter x1, waiting for transfers between devices, on_device(): lax.psum_scatter(grad_w_gate.astype(jnp.bfloat16), ('dp', 'fsdp'), scatte...  104 us
    reduce_scatter x1, waiting for transfers between devices, on_device(): lax.psum_scatter(grad_w_up.astype(jnp.bfloat16), ('dp', 'fsdp'), scatter_...  104 us
    all_gather x1, waiting for transfers between devices, gather_feedforward(): lax.all_gather(w_down, ('dp', 'fsdp'), axis=1, tiled=True)  89.5 us
    unnamed x2, blocking collectives  83.6 us
    dot_general x6, matrix products, block_scores(): jnp.einsum('bij,bh->hij', one_hot, table_local, preferred_element_type=jn...  75.4 us
    reduce_scatter x1, waiting for transfers between devices, on_device(): lax.psum_scatter(ffn_normed_term, 'ctx', scatter_dimension=0, tiled=True)  74.3 us
  transfers between devices with their start and end apart: 24, of which 20 were waited for; matrix products, arithmetic and copies ran while one was open for 23% of the time, Pallas kernels for 0%

commit v1 on v0

--- a/solution.py
+++ b/solution.py
@@ -1,3 +1,4 @@
+import functools
 import jax
 import jax.numpy as jnp
 from jax import lax
@@ -12,6 +13,24 @@
 MASKED = -1e30
 
 
+def cover_signs(original, mesh_name):
+    v_now = lax.axis_index(mesh_name)
+    z2 = lax.axis_size(mesh_name)
+    x_next, arr_out, plain = (z2, v_now, original.shape[0])
+    cards = tuple(((dev_i, (dev_i + 1) % x_next) for dev_i in range(x_next)))
+    y_new = jnp.zeros((*original.shape[:0], x_next * plain, *original.shape[1:]), original.dtype)
+    base_arr = original
+    for w in tuple(range(x_next)):
+        big = (arr_out - w) % x_next
+        y_new = lax.dynamic_update_slice_in_dim(y_new, base_arr, big * plain, axis=0)
+        if w < x_next - 1:
+            base_arr = lax.ppermute(base_arr, mesh_name, cards)
+    return y_new
+
+
+scan_goods = functools.partial(cover_signs, mesh_name=("dp", "fsdp"))
+
+
 def rms_norm(values, gain):
     return values * lax.rsqrt(jnp.mean(values * values, axis=-1, keepdims=True) + EPSILON) * gain
 
@@ -43,7 +62,7 @@
 
 def gather_feedforward(w_gate, w_up, w_down):
     return (
-        lax.all_gather(w_gate, ("dp", "fsdp"), axis=0, tiled=True),
+        scan_goods(w_gate),
         lax.all_gather(w_up, ("dp", "fsdp"), axis=0, tiled=True),
         lax.all_gather(w_down, ("dp", "fsdp"), axis=1, tiled=True),
     )

time: 1930 us -> 1890 us (0.979)
  waiting for transfers between devices: 1090 us -> 1030 us
    ppermute x0 -> x7, waiting for transfers between devices: none -> 142 us  [cover_signs(): base_arr = lax.ppermute(base_arr, mesh_name, cards)]
    all_gather x1, waiting for transfers between devices: 89.5 us -> 0.01 us  [gather_feedforward(): lax.all_gather(w_down, ('dp', 'fsdp'), axis=1, tiled=True)]
    all_gather x1 -> x0, waiting for transfers between devices: 46.1 us -> none  [gather_feedforward(): lax.all_gather(w_gate, ('dp', 'fsdp'), axis=0, tiled=True)]
    reduce_scatter x2, waiting for transfers between devices: 109 us -> 68.1 us  [layer_forward(): lax.psum_scatter(attn_term, 'ctx', scatter_dimension=0, tiled=True)]
    all_gather x1, waiting for transfers between devices: 23.8 us -> 0.01 us  [on_device(): grad_rows = lax.all_gather(cotangent[0], 'ctx', axis=0, tiled=True)]
  transfers between devices with their start and end apart: 24 -> 30, of which waited for: 20 -> 23; matrix products, arithmetic and copies ran while one was open for 23% -> 24% of each run, Pallas kernels for 0% -> 0%
where the time goes in v1:
time: 1890 us; the launch traced here: 1880 us
  waiting for transfers between devices  1030 us (54%)
  matrix products  521 us (28%)
  other arithmetic  126 us (7%)
  blocking collectives  83.7 us (4%)
  loops' own time  53 us (3%)
  local copies, waits for them, and re-layouts  47.8 us (3%)
    dot_general x6, matrix products, block_scores(): jnp.einsum('ihd,jhd->hij', query_block, key_rows, preferred_element_type=...  148 us
    ppermute x7, waiting for transfers between devices, cover_signs(): base_arr = lax.ppermute(base_arr, mesh_name, cards)  142 us
    reduce_scatter x1, waiting for transfers between devices, on_device(): lax.psum_scatter(grad_w_gate.astype(jnp.bfloat16), ('dp', 'fsdp'), scatte...  104 us
    reduce_scatter x1, waiting for transfers between devices, on_device(): lax.psum_scatter(grad_w_up.astype(jnp.bfloat16), ('dp', 'fsdp'), scatter_...  104 us
    unnamed x2, blocking collectives  83.7 us
    dot_general x6, matrix products, block_scores(): jnp.einsum('bij,bh->hij', one_hot, table_local, preferred_element_type=jn...  75.4 us
    reduce_scatter x1, waiting for transfers between devices, on_device(): lax.psum_scatter(ffn_normed_term, 'ctx', scatter_dimension=0, tiled=True)  71.1 us
    reduce_scatter x1, waiting for transfers between devices, on_device(): lax.psum_scatter(grad_w_attn_out.astype(jnp.bfloat16), ('dp', 'fsdp'), sc...  69 us
  transfers between devices with their start and end apart: 30, of which 23 were waited for; matrix products, arithmetic and copies ran while one was open for 24% of the time, Pallas kernels for 0%

profile of v1, /device:TPU:0, one launch (start us, length us, event | category | flops | bytes accessed | tf_op | source)
XLA Modules:
  0.0 1878.9 jit_solution(12106181103794469116)
XLA Ops:
  10.6 43.6 %all-reduce.8 = (bf16[2048]{0:T(1024)(128)(2,1)}, bf16[2048]{0:T(1024)(128)(2,1)S(1)}, bf16[32,32]{1,0:T(8,128)(2,1)S(1)}) all-reduce(bf16[2048]{0:T(1024)(128)(2,1)S(1)} %dynamic-update-slice.2, bf16[2048]{0:T(1024)(128)(2,1)S(1)} %dynamic-update-slice, ...), channel_id=1, replica_groups=mesh['dp'=4,'ctx'=4,'fsdp'=2] {'dp','ctx','fsdp'}, use_global_device_ids=true, to_apply=%add.2 | all-reduce | flops 5120 | bytes 20480
  63.3 35.1 %all-gather.13.cloned.1.call-done = bf16[1024,2048]{1,0:T(8,128)(2,1)} async-done(((bf16[256,2048]{1,0:T(8,128)(2,1)}), bf16[1024,2048]{1,0:T(8,128)(2,1)}) %all-gather.13.cloned.1.call-update) | async-done | bytes 4194320 | tf_op jit(solution)/shard_map/all_gather | solution.py:98
  104.7 45.3 %all-gather.17.cloned.1.call-done = bf16[2048,512]{1,0:T(8,128)(2,1)} async-done(((bf16[256,512]{1,0:T(8,128)(2,1)}), bf16[2048,512]{1,0:T(8,128)(2,1)}) %all-gather.17.cloned.1.call-update) | async-done | bytes 2097168 | tf_op jit(solution)/shard_map/all_gather | solution.py:57
  156.1 43.6 %all-gather.15.cloned.1.call-done = bf16[2048,512]{1,0:T(8,128)(2,1)} async-done(((bf16[256,512]{1,0:T(8,128)(2,1)}), bf16[2048,512]{1,0:T(8,128)(2,1)}) %all-gather.15.cloned.1.call-update) | async-done | bytes 2097168 | tf_op jit(solution)/shard_map/all_gather | solution.py:56
  206.1 128.7 %while.39 = (s32[]{:T(128)}, bf16[2,512,8,64]{1,3,2,0:T(8,128)(2,1)S(1)}, f32[2,8,512,1]{2,1,3,0:T(8,128)S(1)}, s32[2]{0:T(128)S(1)}, s32[1024]{0:T(1024)S(1)}, ...) while((s32[]{:T(128)}, ...), condition=%wide.region_11.12_spmd, body=%wide.region_8.11_spmd.sunk | while | flops 1407709184 | bytes 160060144 | solution.py:130
  238.1 24.2 %fusion.232 = (f32[8,512]{1,0:T(8,128)S(1)}, f32[8,512,1024]{2,1,0:T(8,128)}) fusion(f32[512,1024,8]{1,2,0:T(8,128)} %fusion.231, bf16[1024,8,64]{0,2,1:T(8,128)(2,1)} %get-tuple-element.721, bf16[1024,8,64]{0,2,1:T(8,128)(2,1)} %get-tuple-element.720, s32[]{:T(128)S(6)} %select_n.180, pred[512,1024]{1,0:T(8,128)(4,1)S(1)} %broadcast_compare_fusion.7), kind=kOutput, calls=%fused_computation.192.clone.1 | convolution fusion | flops 549449728 | bytes 35667972 | tf_op jit(solution)/shard_map/while/body/eval_jaxpr/ihd,jhd->hij/dot_general | solution.py:81
  295.2 24.1 %fusion.232 = (f32[8,512]{1,0:T(8,128)S(1)}, f32[8,512,1024]{2,1,0:T(8,128)}) fusion(f32[512,1024,8]{1,2,0:T(8,128)} %fusion.231, bf16[1024,8,64]{0,2,1:T(8,128)(2,1)} %get-tuple-element.721, bf16[1024,8,64]{0,2,1:T(8,128)(2,1)} %get-tuple-element.720, s32[]{:T(128)S(6)} %select_n.180, pred[512,1024]{1,0:T(8,128)(4,1)S(1)} %broadcast_compare_fusion.7), kind=kOutput, calls=%fused_computation.192.clone.1 | convolution fusion | flops 549449728 | bytes 35667972 | tf_op jit(solution)/shard_map/while/body/eval_jaxpr/ihd,jhd->hij/dot_general | solution.py:81
  346.1 68.0 %reduce-scatter.17.cloned.1.call-done = f32[256,2048]{1,0:T(8,128)} async-done(((f32[1024,2048]{1,0:T(8,128)}), f32[256,2048]{1,0:T(8,128)}) %reduce-scatter.17.cloned.1.call-update) | async-done | bytes 2097168 | tf_op jit(solution)/shard_map/reduce_scatter | solution.py:133
  418.0 141.7 %while.38 = (s32[]{:T(128)}, bf16[2,512,8,64]{1,3,2,0:T(8,128)(2,1)S(1)}, s32[2]{0:T(128)S(1)}, s32[1024]{0:T(1024)S(1)}, s32[1,1024]{1,0:T(1,128)S(1)}, /*index...) while((s32[]{:T(128)}, ...), condition=%wide.region_4.5_spmd, body=%wide.region_1.4_spmd.sunk | while | flops 1403525120 | bytes 109630152 | solution.py:130
  435.9 23.7 %fusion.224 = f32[8,512,1024]{2,1,0:T(8,128)} fusion(f32[512,1024,8]{1,2,0:T(8,128)} %fusion.223, bf16[1024,8,64]{0,2,1:T(8,128)(2,1)} %get-tuple-element.763, pred[512,1024]{1,0:T(8,128)(4,1)S(1)} %broadcast_compare_fusion.6, bf16[1024,8,64]{0,2,1:T(8,128)(2,1)} %get-tuple-element.762, s32[]{:T(128)S(6)} %select_n.178), kind=kOutput, calls=%fused_computation.5.clone.1 | convolution fusion | flops 545259520 | bytes 35651588 | tf_op jit(solution)/shard_map/while/body/eval_jaxpr/ihd,jhd->hij/dot_general | solution.py:81
  506.2 23.7 %fusion.224 = f32[8,512,1024]{2,1,0:T(8,128)} fusion(f32[512,1024,8]{1,2,0:T(8,128)} %fusion.223, bf16[1024,8,64]{0,2,1:T(8,128)(2,1)} %get-tuple-element.763, pred[512,1024]{1,0:T(8,128)(4,1)S(1)} %broadcast_compare_fusion.6, bf16[1024,8,64]{0,2,1:T(8,128)(2,1)} %get-tuple-element.762, s32[]{:T(128)S(6)} %select_n.178), kind=kOutput, calls=%fused_computation.5.clone.1 | convolution fusion | flops 545259520 | bytes 35651588 | tf_op jit(solution)/shard_map/while/body/eval_jaxpr/ihd,jhd->hij/dot_general | solution.py:81
  543.9 15.4 fusion.226
  569.6 23.3 %collective-permute-done = bf16[256,1280]{1,0:T(8,128)(2,1)S(1)} collective-permute-done((bf16[256,1280]{1,0:T(8,128)(2,1)S(1)}, bf16[256,1280]{1,0:T(8,128)(2,1)S(1)}, u32[]{:S(2)}, u32[]{:S(2)}) %collective-permute-start) | collective-permute-done | bytes 655392 | tf_op jit(solution)/shard_map/ppermute | solution.py:27
  592.9 33.7 %collective-permute-done.1 = bf16[256,1280]{1,0:T(8,128)(2,1)S(1)} collective-permute-done((bf16[256,1280]{1,0:T(8,128)(2,1)S(1)}, bf16[256,1280]{1,0:T(8,128)(2,1)S(1)}, u32[]{:S(2)}, u32[]{:S(2)}) %collective-permute-start.1) | collective-permute-done | bytes 655392 | tf_op jit(solution)/shard_map/ppermute | solution.py:27
  626.5 33.4 %collective-permute-done.2 = bf16[256,1280]{1,0:T(8,128)(2,1)S(1)} collective-permute-done((bf16[256,1280]{1,0:T(8,128)(2,1)S(1)}, bf16[256,1280]{1,0:T(8,128)(2,1)S(1)}, u32[]{:S(2)}, u32[]{:S(2)}) %collective-permute-start.2) | collective-permute-done | bytes 655392 | tf_op jit(solution)/shard_map/ppermute | solution.py:27
  660.7 15.8 collective-permute-done.3
  742.7 16.7 fusion.77
  778.3 71.1 %reduce-scatter.19.cloned.1.call-done = f32[256,2048]{1,0:T(8,128)} async-done(((f32[1024,2048]{1,0:T(8,128)}), f32[256,2048]{1,0:T(8,128)}) %reduce-scatter.19.cloned.1.call-update) | async-done | bytes 2097168 | tf_op jit(solution)/shard_map/reduce_scatter | solution.py:240
  855.3 34.5 %all-gather.31.cloned.1.call-done = bf16[1024,2048]{1,0:T(8,128)(2,1)} async-done(((bf16[256,2048]{1,0:T(8,128)(2,1)}), bf16[1024,2048]{1,0:T(8,128)(2,1)}) %all-gather.31.cloned.1.call-update) | async-done | bytes 4194320 | tf_op jit(solution)/shard_map/all_gather | solution.py:254
  897.1 214.3 %while.40 = (s32[]{:T(128)}, bf16[2,512,8,64]{1,3,2,0:T(8,128)(2,1)}, f32[2,1024,8,64]{1,3,2,0:T(8,128)}, f32[2,1024,8,64]{1,3,2,0:T(8,128)}, f32[2,32,8]{1,2,0:...) while((s32[]{:T(128)}, ...), condition=%wide.region_18.19_spmd, body=%wide.region_16.18_spmd.sunk | while | flops 3307728896 | bytes 294757248 | solution.py:290
  943.1 25.9 %multiply_reduce_fusion.6 = (f32[8,512]{1,0:T(8,128)S(1)}, f32[8,512,1024]{2,1,0:T(8,128)}) fusion(f32[8,512,1024]{2,1,0:T(8,128)} %fusion.246, f32[8,512]{1,0:T(8,128)S(1)} %dynamic-slice_bitcast_fusion.2, f32[512,1024,8]{1,2,0:T(8,128)} %fusion.248, bf16[1024,8,64]{0,2,1:T(8,128)(2,1)} %get-tuple-element.818, ...), kind=kOutput, calls=%fused_computation.64.clone.1 | convolution fusion | flops 557838336 | bytes 52461572 | tf_op jit(solution)/shard_map/while/body/eval_jaxpr/ihd,jhd->hij/dot_general | solution.py:81
  1037.4 25.9 %multiply_reduce_fusion.6 = (f32[8,512]{1,0:T(8,128)S(1)}, f32[8,512,1024]{2,1,0:T(8,128)}) fusion(f32[8,512,1024]{2,1,0:T(8,128)} %fusion.246, f32[8,512]{1,0:T(8,128)S(1)} %dynamic-slice_bitcast_fusion.2, f32[512,1024,8]{1,2,0:T(8,128)} %fusion.248, bf16[1024,8,64]{0,2,1:T(8,128)(2,1)} %get-tuple-element.818, ...), kind=kOutput, calls=%fused_computation.64.clone.1 | convolution fusion | flops 557838336 | bytes 52461572 | tf_op jit(solution)/shard_map/while/body/eval_jaxpr/ihd,jhd->hij/dot_general | solution.py:81
  1134.8 44.1 %reduce-scatter.21.cloned.1.call-done = bf16[256,2048]{1,0:T(8,128)(2,1)} async-done(((bf16[1024,2048]{1,0:T(8,128)(2,1)}), bf16[256,2048]{1,0:T(8,128)(2,1)}) %reduce-scatter.21.cloned.1.call-update) | async-done | bytes 1048592 | tf_op jit(solution)/shard_map/reduce_scatter | solution.py:318
  1255.0 20.0 %convolution_convert_fusion.3 = bf16[1024,2048]{1,0:T(8,128)(2,1)} fusion(bf16[1280,2048]{1,0:T(8,128)(2,1)} %all-gather.27.cloned.1.call-done, f32[1024,1280]{1,0:T(8,128)} %fusion.120, bf16[1024,2048]{1,0:T(8,128)(2,1)} %all-gather.23.cloned.1.call-done, bf16[2048,1280]{1,0:T(8,128)(2,1)} %all-gather.25.cloned.1.call-done), kind=kOutput, calls=%fused_computation.131 | convolution fusion | flops 10752622592 | bytes 24117248 | tf_op jit(solution)/shard_map/dot_general | solution.py:140
  1275.0 53.3 %reduce-scatter.35.cloned.1.call-done = bf16[1280,256]{1,0:T(8,128)(2,1)} async-done(((bf16[1280,2048]{1,0:T(8,128)(2,1)}), bf16[1280,256]{1,0:T(8,128)(2,1)}) %reduce-scatter.35.cloned.1.call-update) | async-done | bytes 655376 | tf_op jit(solution)/shard_map/reduce_scatter | solution.py:250
  1330.5 103.7 %reduce-scatter.31.cloned.1.call-done = bf16[256,1280]{1,0:T(8,128)(2,1)} async-done(((bf16[2048,1280]{1,0:T(8,128)(2,1)}), bf16[256,1280]{1,0:T(8,128)(2,1)}) %reduce-scatter.31.cloned.1.call-update) | async-done | bytes 655376 | tf_op jit(solution)/shard_map/reduce_scatter | solution.py:244
  1436.5 103.6 %reduce-scatter.33.cloned.1.call-done = bf16[256,1280]{1,0:T(8,128)(2,1)} async-done(((bf16[2048,1280]{1,0:T(8,128)(2,1)}), bf16[256,1280]{1,0:T(8,128)(2,1)}) %reduce-scatter.33.cloned.1.call-update) | async-done | bytes 655376 | tf_op jit(solution)/shard_map/reduce_scatter | solution.py:247
  1542.6 69.0 %reduce-scatter.29.cloned.1.call-done = bf16[512,256]{1,0:T(8,128)(2,1)} async-done(((bf16[512,2048]{1,0:T(8,128)(2,1)}), bf16[512,256]{1,0:T(8,128)(2,1)}) %reduce-scatter.29.cloned.1.call-update) | async-done | bytes 262160 | tf_op jit(solution)/shard_map/reduce_scatter | solution.py:333
  1613.4 68.5 %reduce-scatter.23.cloned.1.call-done = bf16[256,512]{1,0:T(8,128)(2,1)} async-done(((bf16[2048,512]{1,0:T(8,128)(2,1)}), bf16[256,512]{1,0:T(8,128)(2,1)}) %reduce-scatter.23.cloned.1.call-update) | async-done | bytes 262160 | tf_op jit(solution)/shard_map/reduce_scatter | solution.py:324
  1683.7 68.7 %reduce-scatter.27.cloned.1.call-done = bf16[256,512]{1,0:T(8,128)(2,1)} async-done(((bf16[2048,512]{1,0:T(8,128)(2,1)}), bf16[256,512]{1,0:T(8,128)(2,1)}) %reduce-scatter.27.cloned.1.call-update) | async-done | bytes 262160 | tf_op jit(solution)/shard_map/reduce_scatter | solution.py:330
  1754.2 68.5 %reduce-scatter.25.cloned.1.call-done = bf16[256,512]{1,0:T(8,128)(2,1)} async-done(((bf16[2048,512]{1,0:T(8,128)(2,1)}), bf16[256,512]{1,0:T(8,128)(2,1)}) %reduce-scatter.25.cloned.1.call-update) | async-done | bytes 262160 | tf_op jit(solution)/shard_map/reduce_scatter | solution.py:327
  1824.5 40.1 %all-reduce.7 = (f32[2048]{0:T(1024)S(1)}, f32[1024]{0:T(1024)S(1)}, f32[2048]{0:T(1024)S(1)}) all-reduce(f32[2048]{0:T(1024)S(1)} %get-tuple-element.343, f32[1024]{0:T(1024)S(1)} %reshape.387, f32[2048]{0:T(1024)S(1)} %copy-done.34), channel_id=8, replica_groups=mesh['dp'=4,'ctx'=4,'fsdp'=2] {'dp','ctx','fsdp'}, use_global_device_ids=true, to_apply=%region_24.25.clone | all-reduce | flops 5120 | bytes 40960
  (335 shorter events, 544.5 us)
Async XLA Ops:
  7.2 56.2 %all-gather.19.cloned.1.call-start = ((), (), s32[]{:S(2)}) async-start(), calls=%async_computation.15 | async-start | bytes 2359296 | tf_op jit(solution)/shard_map/all_gather | solution.py:58
  7.9 90.6 %all-gather.13.cloned.1.call-start = ((), (), s32[]{:S(2)}) async-start(), calls=%async_computation.12 | async-start | bytes 5242880 | tf_op jit(solution)/shard_map/all_gather | solution.py:98
  59.5 90.5 %all-gather.17.cloned.1.call-start = ((), (), s32[]{:S(2)}) async-start(), calls=%async_computation.14 | async-start | bytes 2359296 | tf_op jit(solution)/shard_map/all_gather | solution.py:57
  60.2 139.5 %all-gather.15.cloned.1.call-start = ((), (), s32[]{:S(2)}) async-start(), calls=%async_computation.13 | async-start | bytes 2359296 | tf_op jit(solution)/shard_map/all_gather | solution.py:56
  60.8 275.4 %all-gather.21.cloned.1.call-start = ((), (), s32[]{:S(2)}) async-start(), calls=%async_computation.16 | async-start | bytes 2359296 | tf_op jit(solution)/shard_map/all_gather | solution.py:59
  61.4 352.8 %reduce-scatter.17.cloned.1.call-start = ((), (), s32[]{:S(2)}) async-start(), calls=%async_computation.22 | async-start | bytes 10485760 | tf_op jit(solution)/shard_map/reduce_scatter | solution.py:133
  343.8 378.9 %all-gather.33.cloned.1.call-start = ((), (), s32[]{:S(2)}) async-start(), calls=%async_computation.34 | async-start | bytes 5242880 | tf_op jit(solution)/shard_map/all_gather | solution.py:221
  344.6 378.2 %all-gather.27.cloned.1.call-start = ((), (), s32[]{:S(2)}) async-start(), calls=%async_computation.20 | async-start | bytes 5898240 | tf_op jit(solution)/shard_map/all_gather | solution.py:67
  345.3 388.0 %all-gather.25.cloned.1.call-start = ((), (), s32[]{:S(2)}) async-start(), calls=%async_computation.19 | async-start | bytes 5898240 | tf_op jit(solution)/shard_map/all_gather | solution.py:66
  346.1 387.3 %all-gather.29.cloned.1.call-start = ((), (), s32[]{:S(2)}) async-start(), calls=%async_computation.23 | async-start | bytes 5242880 | tf_op jit(solution)/shard_map/all_gather | solution.py:135
  417.8 360.5 %reduce-scatter.13.cloned.1.call-start = ((), (), s32[]{:S(2)}) async-start(), calls=%async_computation.17 | async-start | bytes 10485760 | tf_op jit(solution)/shard_map/reduce_scatter | solution.py:133
  567.0 282.4 %reduce-scatter.19.cloned.1.call-start = ((), (), s32[]{:S(2)}) async-start(), calls=%async_computation.24 | async-start | bytes 10485760 | tf_op jit(solution)/shard_map/reduce_scatter | solution.py:240
  568.1 24.8 %collective-permute-start = (bf16[256,1280]{1,0:T(8,128)(2,1)S(1)}, bf16[256,1280]{1,0:T(8,128)(2,1)S(1)}, u32[]{:S(2)}, u32[]{:S(2)}) collective-permute-start(bf16[256,1280]{1,0:T(8,128)(2,1)S(1)} %copy-done.24), channel_id=1, source_target_pairs={{0,1},{1,8},{8,9},{9,16},{16,17},{17,24},{24,25},{25,0},{2,3},{3,1... | collective-permute-start | bytes 1966088 | tf_op jit(solution)/shard_map/ppermute | solution.py:27
  592.9 33.7 %collective-permute-start.1 = (bf16[256,1280]{1,0:T(8,128)(2,1)S(1)}, bf16[256,1280]{1,0:T(8,128)(2,1)S(1)}, u32[]{:S(2)}, u32[]{:S(2)}) collective-permute-start(bf16[256,1280]{1,0:T(8,128)(2,1)S(1)} %collective-permute-done), channel_id=1, source_target_pairs={{0,1},{1,8},{8,9},{9,16},{16,17},{17,24},{24,25},{25,0},{2,3},{3,1... | collective-permute-start | bytes 1966088 | tf_op jit(solution)/shard_map/ppermute | solution.py:27
  626.5 33.4 %collective-permute-start.2 = (bf16[256,1280]{1,0:T(8,128)(2,1)S(1)}, bf16[256,1280]{1,0:T(8,128)(2,1)S(1)}, u32[]{:S(2)}, u32[]{:S(2)}) collective-permute-start(bf16[256,1280]{1,0:T(8,128)(2,1)S(1)} %collective-permute-done.1), channel_id=1, source_target_pairs={{0,1},{1,8},{8,9},{9,16},{16,17},{17,24},{24,25},{25,0},{2,3},{3,1... | collective-permute-start | bytes 1966088 | tf_op jit(solution)/shard_map/ppermute | solution.py:27
  659.9 16.6 collective-permute-start.3
  676.5 15.7 collective-permute-start.4
  692.3 15.0 collective-permute-start.5
  707.2 14.6 collective-permute-start.6
  778.2 111.6 %all-gather.31.cloned.1.call-start = ((), (), s32[]{:S(2)}) async-start(), calls=%async_computation.25 | async-start | bytes 5242880 | tf_op jit(solution)/shard_map/all_gather | solution.py:254
  855.2 323.6 %reduce-scatter.21.cloned.1.call-start = ((), (), s32[]{:S(2)}) async-start(), calls=%async_computation.26 | async-start | bytes 5242880 | tf_op jit(solution)/shard_map/reduce_scatter | solution.py:318
  1134.2 110.3 %all-gather.23.cloned.1.call-start = ((), (), s32[]{:S(2)}) async-start(), calls=%async_computation.18 | async-start | bytes 5242880 | tf_op jit(solution)/shard_map/all_gather | solution.py:135
  1187.2 141.1 %reduce-scatter.35.cloned.1.call-start = ((), (), s32[]{:S(2)}) async-start(), calls=%async_computation.33 | async-start | bytes 5898240 | tf_op jit(solution)/shard_map/reduce_scatter | solution.py:250
  1198.9 235.3 %reduce-scatter.31.cloned.1.call-start = ((), (), s32[]{:S(2)}) async-start(), calls=%async_computation.31 | async-start | bytes 5898240 | tf_op jit(solution)/shard_map/reduce_scatter | solution.py:244
  1208.8 331.2 %reduce-scatter.33.cloned.1.call-start = ((), (), s32[]{:S(2)}) async-start(), calls=%async_computation.32 | async-start | bytes 5898240 | tf_op jit(solution)/shard_map/reduce_scatter | solution.py:247
  1218.7 392.9 %reduce-scatter.29.cloned.1.call-start = ((), (), s32[]{:S(2)}) async-start(), calls=%async_computation.30 | async-start | bytes 2359296 | tf_op jit(solution)/shard_map/reduce_scatter | solution.py:333
  1225.8 456.1 %reduce-scatter.23.cloned.1.call-start = ((), (), s32[]{:S(2)}) async-start(), calls=%async_computation.27 | async-start | bytes 2359296 | tf_op jit(solution)/shard_map/reduce_scatter | solution.py:324
  1231.9 520.4 %reduce-scatter.27.cloned.1.call-start = ((), (), s32[]{:S(2)}) async-start(), calls=%async_computation.29 | async-start | bytes 2359296 | tf_op jit(solution)/shard_map/reduce_scatter | solution.py:330
  1238.2 584.4 %reduce-scatter.25.cloned.1.call-start = ((), (), s32[]{:S(2)}) async-start(), calls=%async_computation.28 | async-start | bytes 2359296 | tf_op jit(solution)/shard_map/reduce_scatter | solution.py:327
  1244.3 625.2 %reduce-scatter.15.cloned.1.call-start = ((), (), s32[]{:S(2)}) async-start(), calls=%async_computation.21 | async-start | bytes 5242880 | tf_op jit(solution)/shard_map/reduce_scatter | solution.py:141
  1275.0 549.5 %copy-start.34 = (f32[2048]{0:T(1024)S(1)}, f32[2048]{0:T(1024)}, u32[]{:S(2)}) copy-start(f32[2048]{0:T(1024)} %get-tuple-element.341) | copy-start | bytes 24580
  1275.0 594.5 %copy-start.9 = (f32[256,2048]{1,0:T(8,128)S(1)}, f32[256,2048]{1,0:T(8,128)}, u32[]{:S(2)}) copy-start(f32[256,2048]{1,0:T(8,128)} %reduce-scatter.13.cloned.1.call-done) | copy-start | bytes 6291460
  (60 other events, 1298.9 us)
Sparse Core Ops, SparseCore 0:
  10.1 53.1 all-gather.18
  65.5 32.9 all-gather.12
  100.6 49.2 all-gather.16
  151.9 47.7 all-gather.14
  201.6 49.5 all-gather.20
  344.0 70.2 reduce-scatter.16
  415.8 34.5 all-gather.32
  452.7 87.2 all-gather.26
  542.3 106.5 all-gather.24
  651.0 43.2 all-gather.28
  697.0 71.6 reduce-scatter.12
  778.3 71.0 reduce-scatter.18
  855.3 34.4 all-gather.30
  1134.3 44.5 reduce-scatter.20
  1187.3 34.4 all-gather.22
  1225.3 102.9 reduce-scatter.34
  1331.7 102.4 reduce-scatter.30
  1437.7 102.3 reduce-scatter.32
  1543.6 68.0 reduce-scatter.28
  1615.0 66.8 reduce-scatter.22
  1685.4 66.8 reduce-scatter.26
  1755.9 66.7 reduce-scatter.24
  1825.2 44.2 reduce-scatter.14
